TPU v7x, 32 devices: a whole 2x2x4 slice. The times are simulated.
32 devices in a mesh: groups: 1, expert: 32 (over z, y, x, core).
Axes of the slice: x: 2, y: 2, z: 4, core: 2. Of those that a mesh axis runs over, the one named last changes fastest.
Arguments:
- tokens: bfloat16 [1024, 4096], P(('groups', 'expert')), may hold values from -6 to 6
- expert_ids: int32 [1024, 8], P(('groups', 'expert')), may hold values from 0 to 15, all different within a row; in each aligned block of 32 rows (0 to 31, 32 to 63, ...) at most 24 rows name the same one
- gate_weights: float32 [1024, 8], P(('groups', 'expert')), may hold values from 0.05 to 0.5
- w_gate: bfloat16 [32, 4096, 384], P('expert'), may hold values from -0.09375 to 0.09375
- w_up: bfloat16 [32, 4096, 384], P('expert'), may hold values from -0.09375 to 0.09375
- w_down: bfloat16 [32, 384, 4096], P('expert'), may hold values from -0.21875 to 0.21875
Outputs:
- moe_out: bfloat16 [1024, 4096], P(('groups', 'expert'))
Inputs may be any that keep to these rules, and one draw needn't show every extreme that they name: `expert_ids`: the 8 experts of a row are distinct. Within the rows of one device (aligned blocks of 32 rows) no expert is named by more than 24 rows, a bound that some block reaches.
All inputs are finite; a program needn't handle non-finite values.
Results may differ from a plain program's by a relative error of at most 0.0067.
Values may be sent and summed in bfloat16 or wider, within the bound.
A program may use at most 128 MiB of HBM per device.

v0:
```python
import jax
import jax.numpy as jnp
from jax import lax
from jax.experimental import pallas as pl
from jax.experimental.pallas import tpu as pltpu
from jax.sharding import PartitionSpec as P

LANES = 128
PLANES = 4
DEVICES = PLANES * 4 * 2
TILE = 512
PIECES = 2


def capacity_of(tok_rows, chosen_count, experts):
    return min(tok_rows, 3 * tok_rows * chosen_count // (2 * experts))


def gathered_kernel(
    tokens, expert_ids, gate_weights, w_gate, w_up, w_down, out,
    rows, gate_mem, up_mem, down_mem, packed, chosen, parts, parts_in,
    second_out, second_in, first_out, first_in, plane_out, plane_in, kept, hidden_mem,
    load_sem, up_send, down_send, plane_recv, first_send, first_recv, second_send, second_recv,
    near_send, near_recv, far_send, far_recv, parts_send, parts_recv,
    back_second_send, back_second_recv, back_first_send, back_first_recv,
    back_plane_send, back_plane_recv,
):
    tok_rows, width = tokens.shape
    wide = width + LANES
    experts = DEVICES // 2
    capacity = capacity_of(tok_rows, expert_ids.shape[0], experts)
    full, pair = 2 * tok_rows, 2 * capacity
    me = lax.axis_index("expert")
    core = lax.rem(me, 2)
    x = lax.rem(me // 2, 2)
    y = lax.rem(me // 4, 2)
    z = me // 8
    expert = me // 2
    along_x, along_y = me + 2 - 4 * x, me + 4 - 8 * y
    first = along_x * (1 - core) + along_y * core
    second = along_y * (1 - core) + along_x * core
    sibling = me + 1 - 2 * core
    above, below = lax.rem(me + 8, DEVICES), lax.rem(me + 24, DEVICES)

    half = z // 2
    low = z + half * (3 - 2 * z)
    planes = [z] + [t + half * (3 - 2 * t) for t in (low + 1, 2 - 2 * low, 3)]

    def remote(src, dst, send, recv, device):
        return pltpu.make_async_remote_copy(
            src_ref=src, dst_ref=dst, send_sem=send, recv_sem=recv,
            device_id={"expert": device}, device_id_type=pl.DeviceIdType.MESH,
        )

    sent = []

    def send(copy):
        copy.start()
        sent.append(copy)

    own = pl.ds(0, tok_rows)
    share_of_width = width // PIECES

    def wide_piece(h):
        return pl.ds(width - share_of_width, share_of_width + LANES) if h == 0 else plain_piece(h)

    def plain_piece(h):
        return pl.ds(width - share_of_width * (h + 1), share_of_width)

    def over_piece(h, body):
        @pl.loop(0, share_of_width // TILE)
        def _(j):
            start = width - share_of_width * (h + 1)
            body(pl.ds(pl.multiple_of(start + j * TILE, TILE), TILE))

    loads = [
        pltpu.make_async_copy(tokens, rows.at[z, core, own, pl.ds(0, width)], load_sem.at[0]),
        pltpu.make_async_copy(w_gate.at[0], gate_mem, load_sem.at[1]),
        pltpu.make_async_copy(w_up.at[0], up_mem, load_sem.at[2]),
        pltpu.make_async_copy(w_down.at[0], down_mem, load_sem.at[3]),
    ]
    for load in loads:
        load.start()

    barrier = pltpu.get_barrier_semaphore()
    partners = [lax.rem(me + 8 * step, DEVICES) for step in (1, 2, 3)] + [first, second, sibling]
    for partner in partners:
        pl.semaphore_signal(
            barrier, inc=1, device_id={"expert": partner}, device_id_type=pl.DeviceIdType.MESH
        )

    ids = jnp.transpose(expert_ids[...])
    gates = jnp.transpose(gate_weights[...])
    lane = lax.broadcasted_iota(jnp.int32, (tok_rows, LANES), 1)
    named = lax.rem(lane, experts)
    weight = jnp.zeros((tok_rows, LANES), jnp.float32)
    member = jnp.zeros((tok_rows, LANES), jnp.float32)
    for k in range(ids.shape[1]):
        same = ids[:, k : k + 1] == named
        weight += jnp.where(same, gates[:, k : k + 1], 0.0)
        member += jnp.where(same, 1.0, 0.0)
    earlier = lax.broadcasted_iota(jnp.int32, (tok_rows, tok_rows), 1) < lax.broadcasted_iota(
        jnp.int32, (tok_rows, tok_rows), 0
    )
    before = jnp.dot(
        jnp.where(earlier, 1.0, 0.0).astype(jnp.bfloat16),
        member.astype(jnp.bfloat16),
        preferred_element_type=jnp.float32,
    )
    high = weight.astype(jnp.bfloat16).astype(jnp.float32)
    beside = jnp.where(lane < experts, high, weight - high)
    beside = jnp.where(lane < 2 * experts, beside, member * (before + 1.0))
    rows[z, core, 0:tok_rows, width:wide] = jnp.where(lane < 3 * experts, beside, 0.0).astype(
        jnp.bfloat16
    )

    loads[0].wait()
    pl.semaphore_wait(barrier, len(partners))

    def column(shares, which):
        at = lax.broadcasted_iota(jnp.int32, shares.shape, 1)
        keep = at == which[0]
        for other in which[1:]:
            keep = keep | (at == other)
        return jnp.sum(jnp.where(keep, shares.astype(jnp.float32), 0.0), axis=1, keepdims=True)

    def plane_copy(q, h, up):
        block = rows.at[q, core, own, wide_piece(h)]
        sems = up_send if up else down_send
        return remote(block, block, sems.at[q, h], plane_recv.at[q, h], above if up else below)

    def pass_on(q, h, act):
        @pl.when((q <= z) & (z < PLANES - 1))
        def _():
            act(plane_copy(q, h, True))

        @pl.when((q >= z) & (z > 0))
        def _():
            act(plane_copy(q, h, False))

    def first_copy(q, h):
        return remote(
            rows.at[q, core, own, wide_piece(h)],
            rows.at[q, core, pl.ds(tok_rows, tok_rows), wide_piece(h)],
            first_send.at[q, h], first_recv.at[q, h], first,
        )

    def second_copy(q, h):
        return remote(
            packed.at[q, :, wide_piece(h)], rows.at[q, core, pl.ds(full, pair), wide_piece(h)],
            second_send.at[q, h], second_recv.at[q, h], second,
        )

    def near_copy(q, h, c):
        block = rows.at[q, c, pl.ds(0, full), wide_piece(h)]
        return remote(block, block, near_send.at[q, h], near_recv.at[q, h], sibling)

    def far_copy(q, h, c):
        block = rows.at[q, c, pl.ds(full, pair), wide_piece(h)]
        return remote(block, block, far_send.at[q, h], far_recv.at[q, h], sibling)

    inner = (z > 0) & (z < PLANES - 1)

    def gather_plane(step, h):
        q = planes[step]
        if step == 1:
            plane_copy(q, h, True).wait_recv()
        if step < 2:
            pass_on(q, h, lambda copy: copy.start())
        else:
            @pl.when(jnp.logical_not(inner))
            def _():
                plane_copy(q, h, True).wait_recv()

        send(first_copy(q, h))

    def gather_early(step, h):
        @pl.when(inner)
        def _():
            plane_copy(planes[step], h, True).wait_recv()
            pass_on(planes[step], h, lambda copy: copy.start())

    def gather_first(step, h):
        q = planes[step]
        first_copy(q, h).wait_recv()
        send(near_copy(q, h, core))
        if h == 0:
            code = column(rows[q, core, 0:full, width:wide], [2 * experts + second // 2])
            row = lax.broadcasted_iota(jnp.int32, (full, pair), 0)
            start = jnp.where(row < tok_rows, 0, capacity)
            place = code.astype(jnp.int32) - 1
            takes = (place >= 0) & (place + start == lax.broadcasted_iota(jnp.int32, (full, pair), 1))
            taken = jnp.where(takes, 1.0, 0.0).astype(jnp.bfloat16)
            chosen[step] = taken
        packed[q, :, wide_piece(h)] = lax.dot_general(
            chosen[step], rows[q, core, 0:full, wide_piece(h)], (((0,), (0,)), ((), ())),
            preferred_element_type=jnp.float32,
        ).astype(jnp.bfloat16)
        send(second_copy(q, h))

    def gather_second(step, h):
        q = planes[step]
        second_copy(q, h).wait_recv()
        send(far_copy(q, h, core))

    def parts_copy(step, h):
        return remote(
            parts.at[step, 1 - core, :, plain_piece(h)], parts_in.at[step, :, plain_piece(h)],
            parts_send.at[step, h], parts_recv.at[step, h], sibling,
        )

    def compute_hidden(step):
        q = planes[step]
        for h in range(PIECES):
            near_copy(q, h, 1 - core).wait_recv()
            far_copy(q, h, 1 - core).wait_recv()
        count = 2 * (full + pair)
        block = rows[q, :, :, 0:width].reshape(count, width)
        gate = jnp.dot(block, gate_mem[...], preferred_element_type=jnp.float32)
        up = jnp.dot(block, up_mem[...], preferred_element_type=jnp.float32)
        hidden_mem[...] = (gate / (1.0 + jnp.exp(-gate)) * up).astype(jnp.bfloat16)

    def compute_parts(step, h):
        def body(columns):
            part = jnp.dot(
                hidden_mem[...], down_mem[:, columns], preferred_element_type=jnp.float32
            )
            parts[step, :, :, columns] = part.astype(jnp.bfloat16).reshape(2, full + pair, TILE)

        over_piece(h, body)
        send(parts_copy(step, h))

    def share_of(step, start, size):
        shares = rows[planes[step], core, start : start + size, width:wide]
        return column(shares, [expert, expert + experts])

    def weighted(step, share, start, columns):
        at = pl.ds(start, share.shape[0])
        both = parts[step, core, at, columns].astype(jnp.float32) + parts_in[
            step, at, columns
        ].astype(jnp.float32)
        return share * both.astype(jnp.bfloat16).astype(jnp.float32)

    def back_second_copy(step, h):
        return remote(
            second_out.at[step, :, plain_piece(h)], second_in.at[step, :, plain_piece(h)],
            back_second_send.at[step, h], back_second_recv.at[step, h], second,
        )

    def back_first_copy(step, h):
        return remote(
            first_out.at[step, :, plain_piece(h)], first_in.at[step, :, plain_piece(h)],
            back_first_send.at[step, h], back_first_recv.at[step, h], first,
        )

    def reduce_parts(step, h):
        share = share_of(step, full, pair)
        parts_copy(step, h).wait_recv()

        def body(columns):
            second_out[step, :, columns] = weighted(step, share, full, columns).astype(jnp.bfloat16)

        over_piece(h, body)
        send(back_second_copy(step, h))

    def reduce_second(step, h):
        share = share_of(step, 0, full)
        back_second_copy(step, h).wait_recv()

        def body(columns):
            back = jnp.dot(
                chosen[step], second_in[step, :, columns], preferred_element_type=jnp.float32
            )
            total = weighted(step, share, 0, columns) + back
            first_out[step, :, columns] = total[tok_rows:].astype(jnp.bfloat16)
            kept[step, :, columns] = total[:tok_rows]

        over_piece(h, body)
        send(back_first_copy(step, h))

    def reduce_first(step, h):
        q = planes[step]
        back_first_copy(step, h).wait_recv()
        if step:

            def body(columns):
                plane_out[step, :, columns] = (
                    kept[step, :, columns] + first_in[step, :, columns].astype(jnp.float32)
                ).astype(jnp.bfloat16)

            over_piece(h, body)
            send(
                remote(
                    plane_out.at[step, :, plain_piece(h)], plane_in.at[z, :, plain_piece(h)],
                    back_plane_send.at[step, h], back_plane_recv.at[z, h],
                    lax.rem(me + 8 * (q - z) + DEVICES, DEVICES),
                )
            )

    gather_plane(0, 0)
    gather_plane(0, 1)
    gather_first(0, 0)
    gather_first(0, 1)
    gather_plane(1, 0)
    gather_early(2, 0)
    gather_plane(1, 1)
    gather_early(2, 1)
    gather_first(1, 0)
    gather_first(1, 1)
    gather_second(0, 0)
    gather_second(0, 1)
    for load in loads[1:]:
        load.wait()
    gather_plane(2, 0)
    gather_plane(2, 1)
    gather_early(3, 0)
    gather_early(3, 1)
    gather_first(2, 0)
    gather_first(2, 1)
    gather_second(1, 0)
    gather_second(1, 1)
    compute_hidden(1)
    gather_plane(3, 0)
    gather_plane(3, 1)
    compute_parts(1, 0)
    compute_parts(1, 1)
    gather_first(3, 0)
    gather_first(3, 1)
    gather_second(2, 0)
    gather_second(2, 1)
    reduce_parts(1, 0)
    reduce_parts(1, 1)
    compute_hidden(2)
    compute_parts(2, 0)
    compute_parts(2, 1)
    gather_second(3, 0)
    gather_second(3, 1)
    reduce_parts(2, 0)
    reduce_parts(2, 1)
    reduce_second(1, 0)
    reduce_second(1, 1)
    compute_hidden(3)
    compute_parts(3, 0)
    compute_parts(3, 1)
    reduce_parts(3, 0)
    reduce_parts(3, 1)
    reduce_first(1, 0)
    reduce_first(1, 1)
    compute_hidden(0)
    compute_parts(0, 0)
    compute_parts(0, 1)
    reduce_second(2, 0)
    reduce_second(2, 1)
    reduce_parts(0, 0)
    reduce_parts(0, 1)
    reduce_second(3, 0)
    reduce_second(3, 1)
    reduce_first(2, 0)
    reduce_first(2, 1)
    reduce_first(3, 0)
    reduce_first(3, 1)
    reduce_second(0, 0)
    reduce_second(0, 1)
    reduce_first(0, 0)
    reduce_first(0, 1)

    for h in range(PIECES):
        for step in (1, 2, 3):
            q = planes[step]
            remote(
                plane_out.at[step, :, plain_piece(h)], plane_in.at[q, :, plain_piece(h)],
                back_plane_send.at[step, h], back_plane_recv.at[q, h], sibling,
            ).wait_recv()

        def finish(columns):
            total = kept[0, :, columns] + first_in[0, :, columns].astype(jnp.float32)
            for step in (1, 2, 3):
                total = total + plane_in[planes[step], :, columns].astype(jnp.float32)
            out[:, columns] = total.astype(jnp.bfloat16)

        over_piece(h, finish)

    for copy in sent:
        copy.wait_send()
    for step in range(PLANES):
        for h in range(PIECES):
            pass_on(planes[step], h, lambda copy: copy.wait_send())


def gathered(tokens, expert_ids, gate_weights, w_gate, w_up, w_down):
    tok_rows, width = tokens.shape
    hidden_units = w_down.shape[1]
    pair = 2 * capacity_of(tok_rows, expert_ids.shape[1], DEVICES // 2)
    full, wide = 2 * tok_rows, width + LANES
    any_spec = pl.BlockSpec(memory_space=pl.ANY)
    vmem_spec = pl.BlockSpec(memory_space=pltpu.VMEM)
    bf16, dma = jnp.bfloat16, pltpu.SemaphoreType.DMA
    return pl.pallas_call(
        gathered_kernel,
        out_shape=jax.ShapeDtypeStruct((tok_rows, width), bf16),
        in_specs=[any_spec, vmem_spec, vmem_spec, any_spec, any_spec, any_spec],
        out_specs=vmem_spec,
        scratch_shapes=[
            pltpu.VMEM((PLANES, 2, full + pair, wide), bf16),
            pltpu.VMEM((width, hidden_units), bf16),
            pltpu.VMEM((width, hidden_units), bf16),
            pltpu.VMEM((hidden_units, width), bf16),
            pltpu.VMEM((PLANES, pair, wide), bf16),
            pltpu.VMEM((PLANES, full, pair), bf16),
            pltpu.VMEM((PLANES, 2, full + pair, width), bf16),
            pltpu.VMEM((PLANES, full + pair, width), bf16),
            pltpu.VMEM((PLANES, pair, width), bf16),
            pltpu.VMEM((PLANES, pair, width), bf16),
            pltpu.VMEM((PLANES, tok_rows, width), bf16),
            pltpu.VMEM((PLANES, tok_rows, width), bf16),
            pltpu.VMEM((PLANES, tok_rows, width), bf16),
            pltpu.VMEM((PLANES, tok_rows, width), bf16),
            pltpu.VMEM((PLANES, tok_rows, width), jnp.float32),
            pltpu.VMEM((2 * (full + pair), hidden_units), bf16),
        ]
        + [dma((PLANES,))]
        + [dma((PLANES, PIECES))] * 19,
        compiler_params=pltpu.CompilerParams(
            collective_id=0, has_side_effects=True, vmem_limit_bytes=60 * 1024 * 1024
        ),
        cost_estimate=pl.CostEstimate(
            flops=6 * DEVICES * tok_rows * width * hidden_units,
            bytes_accessed=6 * width * hidden_units,
            transcendentals=DEVICES * tok_rows * hidden_units,
        ),
    )(tokens, expert_ids.T, gate_weights.T, w_gate, w_up, w_down)


def expert_block(w_gate, w_up, w_down, received):
    sources, count, width = received.shape
    flattened = received.reshape(sources * count, width)
    gate_value = jnp.dot(flattened, w_gate[0], preferred_element_type=jnp.float32)
    up_value = jnp.dot(flattened, w_up[0], preferred_element_type=jnp.float32)
    hidden = (jax.nn.silu(gate_value) * up_value).astype(jnp.bfloat16)
    partial_out = jnp.dot(hidden, w_down[0], preferred_element_type=jnp.float32).astype(
        jnp.bfloat16
    )
    return partial_out.reshape(sources, count, width)


def exchanged(tokens, expert_ids, gate_weights, w_gate, w_up, w_down):
    devices = lax.axis_size("expert")
    experts = devices // 2
    tok_rows, width = tokens.shape
    chosen_count = expert_ids.shape[1]
    capacity = capacity_of(tok_rows, chosen_count, experts)
    one_hot = (expert_ids[:, :, None] == jnp.arange(experts, dtype=jnp.int32)).astype(jnp.int32)
    per_row = jnp.sum(one_hot, axis=1)
    earlier = jnp.cumsum(per_row, axis=0) - per_row
    slot_index = jnp.sum(one_hot * earlier[:, None, :], axis=2)
    position = expert_ids * capacity + slot_index
    row_index = jnp.broadcast_to(jnp.arange(tok_rows, dtype=jnp.int32)[:, None], expert_ids.shape)
    owner = (
        jnp.full((experts * capacity,), tok_rows, jnp.int32)
        .at[position.reshape(-1)]
        .set(row_index.reshape(-1))
    )
    padded = jnp.concatenate([tokens, jnp.zeros((1, width), tokens.dtype)], axis=0)
    selected = padded[owner].reshape(experts, 1, capacity, width)
    outgoing = jnp.broadcast_to(selected, (experts, 2, capacity, width)).reshape(
        devices, capacity, width
    )
    partial_out = expert_block(
        w_gate,
        w_up,
        w_down,
        lax.all_to_all(outgoing, "expert", split_axis=0, concat_axis=0, tiled=True),
    )
    returned = lax.all_to_all(partial_out, "expert", split_axis=0, concat_axis=0, tiled=True)
    paired = returned.reshape(experts, 2, capacity, width).astype(jnp.float32)
    expert_out = (paired[:, 0] + paired[:, 1]).astype(jnp.bfloat16)
    picked = expert_out.reshape(experts * capacity, width)[position]
    mixed = jnp.sum(gate_weights[:, :, None] * picked.astype(jnp.float32), axis=1)
    return mixed.astype(jnp.bfloat16)


def solution(mesh):
    small = mesh.shape["expert"] == DEVICES and mesh.shape["groups"] == 1
    return jax.shard_map(
        gathered if small else exchanged,
        mesh=mesh,
        in_specs=(
            P(("groups", "expert"), None),
            P(("groups", "expert"), None),
            P(("groups", "expert"), None),
            P("expert", None, None),
            P("expert", None, None),
            P("expert", None, None),
        ),
        out_specs=P(("groups", "expert"), None),
        check_vma=False,
    )
```

profile of v0, /device:TPU:0, one launch (start us, length us, event | category | flops | bytes accessed | tf_op | source)
XLA Modules:
  0.0 85.4 jit_solution(11456057273243917619)
XLA Ops:
  0.0 83.7 %shard_map.64 = bf16[32,4096]{1,0:T(8,128)(2,1)} custom-call(bf16[32,4096]{1,0:T(8,128)(2,1)} %tokens.1, s32[8,32]{1,0:T(8,128)} %bitcast.2, f32[8,32]{1,0:T(8,128)} %bitcast.3, bf16[1,4096,384]{2,1,0:T(8,128)(2,1)} %w_gate.1, bf16[1,4096,384]{2,1,0:T(8,128)(2,1)} %w_up.1, bf16[1,384,4096]{2,1,0:T(8,128)(2,1)} %w_down.1), custom_call_target="tpu_custom_call" | custom-call | flops 9663676416 | bytes 9437184 | tf_op jit(solution)/shard_map/pallas_call | solution.py:398
  83.7 1.7 %copy.8 = bf16[32,4096]{1,0:T(8,128)(2,1)} copy(bf16[32,4096]{1,0:T(8,128)(2,1)} %shard_map.64) | data formatting | bytes 524288
where the time goes:
time: 85.6 us; the launch traced here: 85.4 us
  Pallas kernels  83.7 us (98%)
  local copies, waits for them, and re-layouts  1.67 us (2%)
    pallas_call x1, Pallas kernels, gathered(): pl.pallas_call(gathered_kernel, out_shape=jax.ShapeDtypeStruct((tok_rows,...  83.7 us

commit v1 on v0

--- a/solution.py
+++ b/solution.py
@@ -341,8 +341,8 @@
     reduce_second(1, 1)
     compute_hidden(3)
     compute_parts(3, 0)
+    reduce_parts(3, 0)
     compute_parts(3, 1)
-    reduce_parts(3, 0)
     reduce_parts(3, 1)
     reduce_first(1, 0)
     reduce_first(1, 1)
@@ -357,10 +357,10 @@
     reduce_second(3, 1)
     reduce_first(2, 0)
     reduce_first(2, 1)
+    reduce_second(0, 0)
     reduce_first(3, 0)
+    reduce_second(0, 1)
     reduce_first(3, 1)
-    reduce_second(0, 0)
-    reduce_second(0, 1)
     reduce_first(0, 0)
     reduce_first(0, 1)
 

time: 85.6 us -> 86.6 us (1.012)
  Pallas kernels: 83.7 us -> 84.7 us
    pallas_call x1, Pallas kernels: 83.7 us -> 84.7 us  [gathered(): pl.pallas_call(gathered_kernel, out_shape=jax.ShapeDtypeStruct((tok_rows,...]
where the time goes in v1:
time: 86.6 us; the launch traced here: 86.4 us
  Pallas kernels  84.7 us (98%)
  local copies, waits for them, and re-layouts  1.67 us (2%)
    pallas_call x1, Pallas kernels, gathered(): pl.pallas_call(gathered_kernel, out_shape=jax.ShapeDtypeStruct((tok_rows,...  84.7 us

profile of v1, /device:TPU:0, one launch (start us, length us, event | category | flops | bytes accessed | tf_op | source)
XLA Modules:
  0.0 86.4 jit_solution(7481400307365428993)
XLA Ops:
  0.0 84.7 %shard_map.64 = bf16[32,4096]{1,0:T(8,128)(2,1)} custom-call(bf16[32,4096]{1,0:T(8,128)(2,1)} %tokens.1, s32[8,32]{1,0:T(8,128)} %bitcast.2, f32[8,32]{1,0:T(8,128)} %bitcast.3, bf16[1,4096,384]{2,1,0:T(8,128)(2,1)} %w_gate.1, bf16[1,4096,384]{2,1,0:T(8,128)(2,1)} %w_up.1, bf16[1,384,4096]{2,1,0:T(8,128)(2,1)} %w_down.1), custom_call_target="tpu_custom_call" | custom-call | flops 9663676416 | bytes 9437184 | tf_op jit(solution)/shard_map/pallas_call | solution.py:398
  84.7 1.7 %copy.8 = bf16[32,4096]{1,0:T(8,128)(2,1)} copy(bf16[32,4096]{1,0:T(8,128)(2,1)} %shard_map.64) | data formatting | bytes 524288
